TPU v7x, 256 devices: a whole 4x4x8 slice. The times are simulated.
256 devices in a mesh: dp: 16 (over z_lo, y), expert: 16 (over z_hi, x, core).
Axes of the slice: x: 4, y: 4, z: 8 (z_hi: 2, z_lo: 4; z = z_hi * 4 + z_lo), core: 2. Of those that a mesh axis runs over, the one named last changes fastest.
Arguments:
- tokens: bfloat16 [32768, 1024], P(('dp', 'expert')), may hold values from -6 to 6
- grad_out: bfloat16 [32768, 1024], P(('dp', 'expert')), may hold values from -3 to 3
- expert_ids: int32 [32768, 2], P(('dp', 'expert')), may hold values from 0 to 31, all different within a row; in each aligned block of 128 rows (0 to 127, 128 to 255, ...) at most 10 rows name the same one
- gate_values: bfloat16 [32768, 2], P(('dp', 'expert')), may hold values from 0.099609375 to 1
- weight_in: bfloat16 [32, 1024, 4096], P('expert', None, 'dp'), may hold values from -0.1875 to 0.1875
- weight_out: bfloat16 [32, 4096, 1024], P('expert', 'dp'), may hold values from -0.09375 to 0.09375
Outputs:
- grad_tokens: bfloat16 [32768, 1024], P(('dp', 'expert'))
- grad_gates: float32 [32768, 2], P(('dp', 'expert'))
- grad_weight_in: float32 [32, 1024, 4096], P('expert', None, 'dp')
- grad_weight_out: float32 [32, 4096, 1024], P('expert', 'dp')
Inputs may be any that keep to these rules, and one draw needn't show every extreme that they name: `expert_ids`: the 2 experts of one token differ. Among the 128 tokens of one device (aligned blocks of rows in order), no expert is named more than 10 times, a bound that some block reaches.
All inputs are finite; a program needn't handle non-finite values.
Results may differ from a plain program's by a relative error of at most 0.024.
Values may be sent and summed in bfloat16 or wider, within the bound.
A program may use at most 128 MiB of HBM per device.

v0:
```python
import jax
import jax.numpy as jnp
from jax import lax
from jax.sharding import PartitionSpec as P

TOP = 2


GELU_SCALE = 0.7978845608028654
GELU_CUBIC = 0.044715


def slot_positions(route_ids, experts):
    flat_ids = route_ids.reshape(-1)
    onehot = (flat_ids[:, None] == jnp.arange(experts, dtype=jnp.int32)[None, :]).astype(jnp.int32)
    before = jnp.cumsum(onehot, axis=0) - onehot
    return jnp.sum(before * onehot, axis=1).reshape(route_ids.shape)


def expert_piece(shard_piece, weight_in, weight_out):
    routed_x = shard_piece[0][0]
    routed_dy = shard_piece[1][0]
    routed_gate = shard_piece[2][0]
    hidden_pre = jnp.einsum("lrd,ldf->lrf", routed_x, weight_in, preferred_element_type=jnp.float32)
    tanh_part = jnp.tanh(
        GELU_SCALE * (hidden_pre + GELU_CUBIC * hidden_pre * hidden_pre * hidden_pre)
    )
    activated = (0.5 * hidden_pre * (1.0 + tanh_part)).astype(jnp.bfloat16)
    upstream = jnp.einsum("lrd,lfd->lrf", routed_dy, weight_out, preferred_element_type=jnp.float32)
    gate_part = jnp.sum(activated * upstream, axis=2).T
    slope = 0.5 * (1.0 + tanh_part) + 0.5 * hidden_pre * (
        1.0 - tanh_part * tanh_part
    ) * GELU_SCALE * (1.0 + 3.0 * GELU_CUBIC * hidden_pre * hidden_pre)
    gate_col = routed_gate.astype(jnp.float32)[:, :, None]
    grad_hidden = (gate_col * upstream * slope).astype(jnp.bfloat16)
    scaled_dy = (gate_col * routed_dy).astype(jnp.bfloat16)
    grad_in = jnp.einsum("lrd,lrf->ldf", routed_x, grad_hidden, preferred_element_type=jnp.float32)
    grad_out_w = jnp.einsum(
        "lrf,lrd->lfd", activated, scaled_dy, preferred_element_type=jnp.float32
    )
    return (grad_in, grad_out_w, grad_hidden, gate_part)


def per_device(tokens, grad_out, expert_ids, gate_values, weight_in, weight_out):
    tok_dev, model_width = tokens.shape
    local_experts = weight_in.shape[0]
    expert_count = lax.axis_size("expert")
    experts = local_experts * expert_count
    capacity = TOP * tok_dev * 5 // (4 * experts)
    slot_total = experts * capacity
    positions = slot_positions(expert_ids, experts)
    slot_index = expert_ids * capacity + positions
    slot_iota = jnp.arange(slot_total, dtype=jnp.int32)
    selector = slot_index[:, :, None] == slot_iota[None, None, :]
    spread_matrix = jnp.sum(selector.astype(jnp.int32), axis=1).astype(jnp.bfloat16)
    slot_x = jnp.einsum(
        "ts,td->sd", spread_matrix, tokens, preferred_element_type=jnp.float32
    ).astype(jnp.bfloat16)
    slot_dy = jnp.einsum(
        "ts,td->sd", spread_matrix, grad_out, preferred_element_type=jnp.float32
    ).astype(jnp.bfloat16)
    slot_gate = jnp.einsum(
        "tks,tk->s",
        selector.astype(jnp.float32),
        gate_values.astype(jnp.float32),
        precision=lax.Precision.HIGHEST,
    ).astype(jnp.bfloat16)
    slot_shape = (expert_count, local_experts, capacity, model_width)
    arrived = (
        lax.all_to_all(
            slot_x.reshape(slot_shape), "expert", split_axis=0, concat_axis=2, tiled=True
        ),
        lax.all_to_all(
            slot_dy.reshape(slot_shape), "expert", split_axis=0, concat_axis=2, tiled=True
        ),
        lax.all_to_all(
            slot_gate.reshape(expert_count, local_experts, capacity),
            "expert",
            split_axis=0,
            concat_axis=2,
            tiled=True,
        ),
    )
    gathered = (
        lax.all_gather(arrived[0], "dp", axis=2, tiled=True),
        lax.all_gather(arrived[1], "dp", axis=2, tiled=True),
        lax.all_gather(arrived[2], "dp", axis=2, tiled=True),
    )
    running = expert_piece(gathered, weight_in, weight_out)
    grad_in, grad_out_w, hidden_store, gate_store = running
    token_part = lax.psum_scatter(
        jnp.einsum(
            "lrf,ldf->rld", hidden_store, weight_in, preferred_element_type=jnp.float32
        ).astype(jnp.bfloat16),
        "dp",
        scatter_dimension=0,
        tiled=True,
    ).astype(jnp.float32)
    gate_mine = lax.psum_scatter(gate_store, "dp", scatter_dimension=0, tiled=True)
    back_dx, back_gate = (
        lax.all_to_all(
            token_part.reshape(expert_count, capacity, local_experts, model_width).astype(
                jnp.bfloat16
            ),
            "expert",
            split_axis=0,
            concat_axis=0,
            tiled=True,
        ).astype(jnp.float32),
        lax.all_to_all(
            gate_mine.reshape(expert_count, capacity, local_experts).astype(jnp.bfloat16),
            "expert",
            split_axis=0,
            concat_axis=0,
            tiled=True,
        ).astype(jnp.float32),
    )
    flat_index = (
        expert_ids // local_experts * capacity + positions
    ) * local_experts + expert_ids % local_experts
    combiner = (flat_index[:, :, None] == slot_iota[None, None, :]).astype(jnp.float32)
    grad_tokens = jnp.einsum(
        "tks,sd->td",
        combiner,
        back_dx.reshape(slot_total, model_width),
        precision=lax.Precision.HIGHEST,
        preferred_element_type=jnp.float32,
    ).astype(jnp.bfloat16)
    grad_gates = jnp.einsum(
        "tks,s->tk", combiner, back_gate.reshape(slot_total), precision=lax.Precision.HIGHEST
    )
    return (grad_tokens, grad_gates, grad_in, grad_out_w)


def solution(mesh):
    placed = (
        P(("dp", "expert"), None),
        P(("dp", "expert"), None),
        P(("dp", "expert"), None),
        P(("dp", "expert"), None),
        P("expert", None, "dp"),
        P("expert", "dp", None),
    )
    return jax.shard_map(
        per_device,
        mesh=mesh,
        in_specs=placed,
        out_specs=(
            P(("dp", "expert"), None),
            P(("dp", "expert"), None),
            P("expert", None, "dp"),
            P("expert", "dp", None),
        ),
        check_vma=False,
    )
```

profile of v0, /device:TPU:1, one launch (start us, length us, event | category | flops | bytes accessed | tf_op | source)
XLA Modules:
  0.0 570.8 jit_solution(3721467956894439177)
XLA Ops:
  7.2 0.9 copy.97
  8.1 0.1 eq.57
  8.3 0.1 eq.53
  8.4 0.6 reduce-window.6
  9.0 0.2 slice_reduce_fusion
  9.2 0.1 fusion.25
  9.4 0.1 reshape.57
  9.6 0.7 multiply_add_fusion.1
  10.3 1.3 convolution_convert_fusion
  11.6 0.2 reshape.60
  11.8 0.7 copy.107
  12.5 29.1 %all_to_all.64 = bf16[16,2,10,1024]{3,1,2,0:T(2,128)(2,1)S(1)} all-to-all(bf16[16,2,10,1024]{3,1,2,0:T(2,128)(2,1)S(1)} %copy.107), channel_id=1, replica_groups=mesh['dp'=16,'expert'=16] {'expert'}, dimensions={0} | all-to-all | bytes 1310720 | tf_op jit(solution)/shard_map/all_to_all | solution.py:70
  41.7 1.0 copy.108
  42.7 0.3 convolution_convert_fusion.1
  43.1 0.2 reshape.59
  43.3 0.7 copy.105
  44.0 25.1 %all_to_all.65 = bf16[16,2,10,1024]{3,1,2,0:T(2,128)(2,1)S(1)} all-to-all(bf16[16,2,10,1024]{3,1,2,0:T(2,128)(2,1)S(1)} %copy.105), channel_id=1, replica_groups=mesh['dp'=16,'expert'=16] {'expert'}, dimensions={0} | all-to-all | bytes 1310720 | tf_op jit(solution)/shard_map/all_to_all | solution.py:73
  69.0 1.0 copy.106
  70.1 0.2 convolution_reduce_fusion
  70.3 0.1 reshape.58
  70.4 13.1 %all_to_all.66 = bf16[16,2,10]{2,1,0:T(2,128)(2,1)S(1)} all-to-all(bf16[16,2,10]{2,1,0:T(2,128)(2,1)S(1)} %reshape.58), channel_id=1, replica_groups=mesh['dp'=16,'expert'=16] {'expert'}, dimensions={0} | all-to-all | bytes 1280 | tf_op jit(solution)/shard_map/all_to_all | solution.py:76
  83.5 0.1 all_to_all.48
  83.6 0.2 copy.103
  83.8 116.4 %all_gather.9 = bf16[1,2,2560]{1,0,2:T(2,128)(2,1)S(1)} all-gather(bf16[1,2,160]{1,0,2:T(2,128)(2,1)S(1)} %copy.103), channel_id=1, replica_groups=mesh['dp'=16,'expert'=16] {'dp'}, dimensions={2}, use_global_device_ids=true | all-gather | bytes 10880 | tf_op jit(solution)/shard_map/all_gather | solution.py:87
  200.2 1.4 convert_element_type.95
  201.6 0.4 copy.104
  202.0 12.8 %fusion.3 = f32[2,2560,256]{1,2,0:T(8,128)} fusion(bf16[2,1024,256]{2,1,0:T(8,128)(2,1)S(1)} %copy-done, bf16[1,2,2560,1024]{3,2,1,0:T(8,128)(2,1)} %all-gather.5.cloned.1.call-done), kind=kOutput, calls=%fused_computation.4 | convolution fusion | flops 2684354560 | bytes 16777216 | tf_op jit(solution)/shard_map/lrd,ldf->lrf/dot_general | solution.py:24
  214.8 99.1 %all-gather.3.cloned.1.call-done = bf16[1,2,2560,1024]{3,2,1,0:T(8,128)(2,1)} async-done(((bf16[1,2,160,1024]{3,2,1,0:T(8,128)(2,1)}), bf16[1,2,2560,1024]{3,2,1,0:T(8,128)(2,1)}) %all-gather.3.cloned.1.call-update) | async-done | bytes 10485776 | tf_op jit(solution)/shard_map/all_gather | solution.py:86
  313.8 10.9 %multiply_reduce_fusion = (f32[2,2560]{1,0:T(2,128)S(1)}, bf16[2,2560,256]{1,2,0:T(8,128)(2,1)}) fusion(f32[2,2560,256]{1,2,0:T(8,128)} %fusion.3, f32[2,2560]{1,0:T(2,128)S(1)} %copy.104, bf16[2,256,1024]{2,1,0:T(8,128)(2,1)S(1)} %copy-done.3, bf16[1,2,2560,1024]{3,2,1,0:T(8,128)(2,1)} %all-gather.3.cloned.1.call-done), kind=kOutput, calls=%fused_computation.20 | convolution fusion | flops 2717117440 | bytes 19439616 | tf_op jit(solution)/shard_map/lrd,lfd->lrf/dot_general | solution.py:29
  324.7 1.5 copy.123
  326.3 0.2 reduce-scatter.5.cloned.1.call-start
  326.5 8.3 %convert_bitcast_fusion = bf16[2560,2,1024]{2,0,1:T(8,128)(2,1)} fusion(bf16[2,2560,256]{1,2,0:T(8,128)(2,1)} %get-tuple-element.5, bf16[2,1024,256]{2,1,0:T(8,128)(2,1)S(1)} %copy-done), kind=kOutput, calls=%fused_computation.10 | convolution fusion | flops 2689597440 | bytes 14155776 | tf_op jit(solution)/shard_map/lrf,ldf->rld/dot_general | solution.py:92
  334.8 62.9 %reduce-scatter.7.cloned.1.call-done = f32[160,2]{1,0:T(8,128)} async-done(((f32[2560,2]{1,0:T(8,128)}), f32[160,2]{1,0:T(8,128)}) %reduce-scatter.7.cloned.1.call-update) | async-done | bytes 1296
  397.7 0.9 convert_element_type.96
  398.6 0.1 copy.126
  398.7 0.1 convert_element_type.92
  398.8 0.6 copy.112
  399.4 18.3 %all-to-all-start.4 = ((bf16[16,10,2]{1,2,0:T(2,128)(2,1)}), bf16[16,10,2]{1,2,0:T(2,128)(2,1)S(1)}, u32[]{:S(2)}, u32[]{:S(2)}) async-start(bf16[16,10,2]{1,2,0:T(2,128)(2,1)} %copy.112), calls=%async_computation.5 | async-start | bytes 16384 | tf_op jit(solution)/shard_map/all_to_all | solution.py:110
  417.7 113.3 %reduce-scatter.5.cloned.1.call-done = bf16[160,2,1024]{2,0,1:T(8,128)(2,1)} async-done(((bf16[2560,2,1024]{2,0,1:T(8,128)(2,1)}), bf16[160,2,1024]{2,0,1:T(8,128)(2,1)}) %reduce-scatter.5.cloned.1.call-update) | async-done | bytes 655376 | tf_op jit(solution)/shard_map/reduce_scatter | solution.py:91
  531.0 2.6 copy.111
  533.6 7.4 %all-to-all-start.3 = ((bf16[16,10,2,1024]{3,2,1,0:T(2,128)(2,1)}), bf16[16,10,2,1024]{3,2,1,0:T(2,128)(2,1)S(1)}, u32[]{:S(2)}, u32[]{:S(2)}) async-start(bf16[16,10,2,1024]{3,2,1,0:T(2,128)(2,1)} %bitcast.14), calls=%async_computation.4 | async-start | bytes 1310720 | tf_op jit(solution)/shard_map/all_to_all | solution.py:101
  541.0 11.0 %fusion = f32[2,256,1024]{2,1,0:T(8,128)} fusion(bf16[1,2,2560,1024]{3,2,1,0:T(8,128)(2,1)} %all-gather.3.cloned.1.call-done, f32[2,2560]{1,0:T(2,128)S(1)} %copy.104, f32[2,2560,256]{1,2,0:T(8,128)} %fusion.3), kind=kOutput, calls=%fused_computation.1 | convolution fusion | flops 2711879680 | bytes 17846272 | tf_op jit(solution)/shard_map/lrf,lrd->lfd/dot_general | solution.py:38
  552.1 9.6 %fusion.1 = f32[2,1024,256]{2,1,0:T(8,128)} fusion(bf16[2,2560,256]{1,2,0:T(8,128)(2,1)S(1)} %copy-done.1, bf16[1,2,2560,1024]{3,2,1,0:T(8,128)(2,1)} %all-gather.5.cloned.1.call-done), kind=kOutput, calls=%fused_computation.2 | convolution fusion | flops 2684354560 | bytes 15204352 | tf_op jit(solution)/shard_map/lrd,lrf->ldf/dot_general | solution.py:37
  561.6 0.2 copy.113
  561.8 0.1 reshape.66
  562.0 0.7 fusion.17
  562.7 0.2 reshape.61
  563.0 1.3 convolution_convert_fusion.2
  (27 shorter events, 0.4 us)
Async XLA Ops:
  7.2 194.8 %copy-start = (bf16[2,1024,256]{2,1,0:T(8,128)(2,1)S(1)}, bf16[2,1024,256]{2,1,0:T(8,128)(2,1)}, u32[]{:S(2)}) copy-start(bf16[2,1024,256]{2,1,0:T(8,128)(2,1)} %param.10) | copy-start | bytes 3145732
  7.2 35.6 %copy-start.2 = (bf16[128,1024]{1,0:T(8,128)(2,1)S(1)}, bf16[128,1024]{1,0:T(8,128)(2,1)}, u32[]{:S(2)}) copy-start(bf16[128,1024]{1,0:T(8,128)(2,1)} %param.7) | copy-start | bytes 786436
  7.2 194.8 %all-gather.5.cloned.1.call-start = ((), (), s32[]{:S(2)}) async-start(), calls=%async_computation.8 | async-start | bytes 11141120 | tf_op jit(solution)/shard_map/all_gather | solution.py:85
  12.5 57.6 %copy-start.4 = (bf16[128,2]{0,1:T(2,128)(2,1)S(1)}, bf16[128,2]{0,1:T(2,128)(2,1)}, u32[]{:S(2)}) copy-start(bf16[128,2]{0,1:T(2,128)(2,1)} %param.9) | copy-start | bytes 1540
  42.7 271.2 %all-gather.3.cloned.1.call-start = ((), (), s32[]{:S(2)}) async-start(), calls=%async_computation.7 | async-start | bytes 11141120 | tf_op jit(solution)/shard_map/all_gather | solution.py:86
  70.1 327.6 %reduce-scatter.7.cloned.1.call-start = ((), (), s32[]{:S(2)}) async-start(), calls=%async_computation.10 | async-start | bytes 1392640
  202.0 111.9 %copy-start.3 = (bf16[2,256,1024]{2,1,0:T(8,128)(2,1)S(1)}, bf16[2,256,1024]{2,1,0:T(8,128)(2,1)}, u32[]{:S(2)}) copy-start(bf16[2,256,1024]{2,1,0:T(8,128)(2,1)} %param.11) | copy-start | bytes 3145732
  326.3 204.8 %reduce-scatter.5.cloned.1.call-start = ((), (), s32[]{:S(2)}) async-start(), calls=%async_computation.9 | async-start | bytes 11141120 | tf_op jit(solution)/shard_map/reduce_scatter | solution.py:91
  399.4 134.2 %all-to-all-start.4 = ((bf16[16,10,2]{1,2,0:T(2,128)(2,1)}), bf16[16,10,2]{1,2,0:T(2,128)(2,1)S(1)}, u32[]{:S(2)}, u32[]{:S(2)}) async-start(bf16[16,10,2]{1,2,0:T(2,128)(2,1)} %copy.112), calls=%async_computation.5 | async-start | bytes 16384 | tf_op jit(solution)/shard_map/all_to_all | solution.py:110
  533.6 29.1 %all-to-all-start.3 = ((bf16[16,10,2,1024]{3,2,1,0:T(2,128)(2,1)}), bf16[16,10,2,1024]{3,2,1,0:T(2,128)(2,1)S(1)}, u32[]{:S(2)}, u32[]{:S(2)}) async-start(bf16[16,10,2,1024]{3,2,1,0:T(2,128)(2,1)} %bitcast.14), calls=%async_computation.4 | async-start | bytes 1310720 | tf_op jit(solution)/shard_map/all_to_all | solution.py:101
  541.0 11.0 %copy-start.1 = (bf16[2,2560,256]{1,2,0:T(8,128)(2,1)S(1)}, bf16[2,2560,256]{1,2,0:T(8,128)(2,1)}, u32[]{:S(2)}) copy-start(bf16[2,2560,256]{1,2,0:T(8,128)(2,1)} %get-tuple-element.5) | copy-start | bytes 7864324
Sparse Core Ops, SparseCore 0:
  42.8 144.2 all-gather.4
  189.5 124.2 all-gather.2
  326.4 71.2 reduce-scatter.6
  400.1 130.8 reduce-scatter.4
where the time goes:
time: 571 us
  waiting for transfers between devices  275 us (48%)
  blocking collectives  184 us (32%)
  matrix products  56.4 us (10%)
  starting transfers between devices  26 us (5%)
  between operations  14 us (2%)
  local copies, waits for them, and re-layouts  11.6 us (2%)
    all_gather x1, blocking collectives, per_device(): lax.all_gather(arrived[2], 'dp', axis=2, tiled=True)  116 us
    reduce_scatter x1, waiting for transfers between devices, per_device(): lax.psum_scatter(jnp.einsum('lrf,ldf->rld', hidden_store, weight_in, pref...  113 us
    all_gather x1, waiting for transfers between devices, per_device(): lax.all_gather(arrived[1], 'dp', axis=2, tiled=True)  99.1 us
    unnamed x5, waiting for transfers between devices  63 us
    all_to_all x1, blocking collectives, per_device(): lax.all_to_all(slot_x.reshape(slot_shape), 'expert', split_axis=0, concat...  29.1 us
    all_to_all x1, blocking collectives, per_device(): lax.all_to_all(slot_dy.reshape(slot_shape), 'expert', split_axis=0, conca...  25.1 us
    all_to_all x1, starting transfers between devices, per_device(): lax.all_to_all(gate_mine.reshape(expert_count, capacity, local_experts).a...  18.3 us
    all_to_all x1, blocking collectives, per_device(): lax.all_to_all(slot_gate.reshape(expert_count, local_experts, capacity),...  13.1 us
  transfers between devices with their start and end apart: 6, of which 3 were waited for; matrix products, arithmetic and copies ran while one was open for 9% of the time, Pallas kernels for 0%

commit v1 on v0

v1 whole, which is shorter than its diff:
```python
import functools

import jax
import jax.numpy as jnp
from jax import lax
from jax.experimental import pallas as pl
from jax.experimental.pallas import tpu as pltpu
from jax.sharding import PartitionSpec as P

MESH = pl.DeviceIdType.MESH
BF, F32 = jnp.bfloat16, jnp.float32
GELU_SCALE = 0.7978845608028654
GELU_CUBIC = 0.044715

D = 1024
HID = 256
TOK = 128
CAP = 10
ROWS = 8 * CAP
RET = 48

PLACE = {0: 0, 1: 1, 7: 2, 2: 3, 6: 4, 3: 5, 5: 6, 4: 7}
ORDER = (1, 7, 2, 6, 3, 5, 4)


def dot(a, b):
    return lax.dot_general(a, b, (((1,), (0,)), ((), ())), preferred_element_type=F32)


def dot_nt(a, b):
    return lax.dot_general(a, b, (((1,), (1,)), ((), ())), preferred_element_type=F32)


def dot_tn(a, b):
    return lax.dot_general(a, b, (((0,), (0,)), ((), ())), preferred_element_type=F32)


def iota(shape, dim):
    return lax.broadcasted_iota(jnp.int32, shape, dim)


def kernel(
    tok, gout, meta, win, wout,
    gtok_o, ggate_o, gwin_o, gwout_o,
    raw, meta_far, ms, mr, xs, ds, xo, do,
    wi, wo, act, dpre, dtacc, gacc, dt, rb, gp, gr,
    dwi, dwo, yri, yro, fin_li, fin_lo, fin_ri, fin_ro,
    pack, rets, retr,
    core_s, core_r, loc_s, xs_s, xs_r, zx_s, zx_r, zf_s, zo_s, ya_s, ya_r,
    zb_s, zb_r, gt_s, gt_r, yb_s, yb_r, rt_s, rt_r,
):
    dp, ex = lax.axis_index("dp"), lax.axis_index("expert")
    zl, y = dp // 4, dp % 4
    zh, x, c = ex // 8, (ex // 2) % 4, ex % 2
    z = zh * 4 + zl

    def dev(dz=0, dy=0, dx=0, dc=0):
        zz, yy, xx, cc = (z + dz + 8) % 8, (y + dy + 4) % 4, (x + dx + 4) % 4, (c + dc) % 2
        return ((zz % 4) * 4 + yy, (zz // 4) * 8 + xx * 2 + cc)

    def remote(src, dst, send, recv, to):
        return pltpu.make_async_remote_copy(
            src_ref=src, dst_ref=dst, send_sem=send, recv_sem=recv, device_id=to, device_id_type=MESH
        )

    barrier = pltpu.get_barrier_semaphore()
    partners = [dev(dz=k) for k in range(1, 8)] + [dev(dy=1), dev(dy=3)]
    partners += [dev(dx=k, dc=j) for k in range(4) for j in range(2) if k or j]
    for to in partners:
        pl.semaphore_signal(barrier, inc=1, device_id=to, device_id_type=MESH)
    pl.semaphore_wait(barrier, len(partners))

    sent = []

    def start(copy):
        copy.start()
        sent.append(copy)
        return copy

    right, left = dev(dy=1), dev(dy=3)

    def y_gather(e, kind):
        src = {
            "i_r": (win.at[e], wi.at[e, 3], right, 0),
            "o_r": (wout.at[e], wo.at[e, 3], right, 1),
            "i_l": (win.at[e], wi.at[e, 1], left, 2),
            "o_l": (wout.at[e], wo.at[e, 1], left, 3),
            "i_f": (wi.at[e, 3], wi.at[e, 2], right, 4),
            "o_f": (wo.at[e, 1], wo.at[e, 2], left, 5),
        }[kind]
        return remote(src[0], src[1], ya_s.at[e, src[3]], ya_r.at[e, src[3]], src[2])

    def y_own(e):
        for kind in ("i_r", "o_l", "o_r", "i_l"):
            start(y_gather(e, kind))

    def y_forward(e):
        y_gather(e, "i_r").wait_recv()
        start(y_gather(e, "i_f"))
        y_gather(e, "o_l").wait_recv()
        start(y_gather(e, "o_f"))

    def y_rest(e):
        for kind in ("o_r", "i_l", "i_f", "o_f"):
            y_gather(e, kind).wait_recv()

    y_own(0)
    core = dev(dc=1)
    swaps = [
        remote(meta, meta_far, core_s.at[0], core_r.at[0], core),
        remote(tok, raw.at[pl.ds(TOK, TOK)], core_s.at[1], core_r.at[1], core),
        remote(gout, raw.at[pl.ds(3 * TOK, TOK)], core_s.at[2], core_r.at[2], core),
    ]
    for copy in swaps:
        start(copy)
    local = []
    for e in range(2):
        local.append(pltpu.make_async_copy(win.at[e], wi.at[e, 0], loc_s.at[e, 0]))
        local.append(pltpu.make_async_copy(wout.at[e], wo.at[e, 0], loc_s.at[e, 1]))
    for copy in local:
        copy.start()

    raw[0:TOK, :] = tok[...]
    raw[2 * TOK : 3 * TOK, :] = gout[...]
    gp[...] = jnp.zeros_like(gp)
    before = (iota((TOK, TOK), 0) < iota((TOK, TOK), 1)).astype(F32).astype(BF)

    def ranks(ids0, ids1, wanted):
        hit0, hit1 = ids0 == wanted, ids1 == wanted
        hit = jnp.where(hit0 | hit1, 1.0, 0.0)
        return hit, dot(hit.astype(BF), before), hit0, hit1

    number = iota((32, TOK), 0)
    own0, own1 = meta[0:1, :], meta[1:2, :]
    _, own_rank, hit0, hit1 = ranks(own0, own1, number.astype(F32))
    num_ex = number >> 1
    xr = (((num_ex >> 1) & 3) - x + 4) & 3
    cr = (num_ex + c) & 1
    zr = ((num_ex >> 3) + zh) & 1
    message = (xr * 2 + cr) * RET
    row_code = (message + zr * 20 + (number & 1) * 10).astype(F32) + own_rank
    gate_code = (message + 40 + zr * 2 + (number & 1)).astype(F32)
    lane_code = (((4 - xr) & 3) * 20 + cr * 10).astype(F32) + own_rank

    def pick(hit, table):
        return jnp.sum(jnp.where(hit, table, 0.0), axis=0, keepdims=True).astype(jnp.int32)

    home = [[pick(hit, t) for t in (row_code, gate_code, lane_code)] for hit in (hit0, hit1)]

    for copy in swaps:
        copy.wait_recv()

    k = iota((16, TOK), 0)
    k_x, k_zone, k_e = (x + ((k >> 1) & 3)) & 3, (zh + (k & 1)) & 1, k >> 3
    wanted = ((k_zone * 8 + k_x * 2 + c) * 2 + k_e).astype(F32)
    codes, gates = [], []
    for side, m in enumerate((meta, meta_far)):
        hit, rank, h0, h1 = ranks(m[0:1, :], m[1:2, :], wanted)
        codes.append(jnp.where(hit > 0.0, rank + side * CAP, -1.0))
        gates.append(jnp.where(h0, m[2:3, :], 0.0) + jnp.where(h1, m[3:4, :], 0.0))
    far = [jnp.where(v >= 0.0, v + 20.0, -1.0) for v in codes]
    code = jnp.concatenate(codes + far, axis=1).astype(jnp.int32)
    weight = jnp.concatenate([jnp.ones((16, 2 * TOK), F32)] + gates, axis=1)

    def x_send(e, k):
        return remote(
            ms.at[e, pl.ds(k * 80, 80)], mr.at[e, pl.ds((4 - k) % 4 * 80, 80)],
            xs_s.at[e, k], xs_r.at[e, k], dev(dx=k),
        )

    def dispatch(e):
        blocks = []
        for k in range(8):
            at = e * 8 + k
            same = iota((40, 4 * TOK), 0) == code[at : at + 1, :]
            blocks.append(jnp.where(same, weight[at : at + 1, :], 0.0))
        spread = jnp.concatenate(blocks, axis=0).astype(BF)
        rows = dot(spread, raw[...]).astype(BF)
        ms[e] = rows
        for k in (1, 3, 2):
            start(x_send(e, k))
        mr[e, 0:80, :] = rows[0:80, :]

    dispatch(0)
    dispatch(1)

    o, i = iota((320, 320), 0), iota((320, 320), 1)
    oa, ia = o // 20, i // 20
    unpack = ((o - oa * 20 == i - ia * 20) & ((oa & 3) == (ia >> 2)) & ((oa >> 2) == (ia & 3)))
    unpack = unpack.astype(F32).astype(BF)

    def arrive(e):
        for k in (1, 3, 2):
            x_send(e, k).wait_recv()
        rows = dot(unpack, mr[e]).astype(BF)
        xs[e, 0:80, :] = rows[0:80, :]
        ds[e, 0:80, :] = rows[80:160, :]
        xo[e] = rows[160:240, :]
        do[e] = rows[240:320, :]

    def place(at):
        return pl.ds(at * ROWS, ROWS)

    def z_copy(e, part, src, at, to, send):
        where = (xs, ds)[part]
        return remote(src, where.at[e, place(at)], send, zx_r.at[e, part, at], to)

    cond_sent = []

    def z_own(e):
        for part in range(2):
            mine = (xs, ds)[part].at[e, place(0)]

            def go(way, rho, dz):
                return z_copy(e, part, mine, PLACE[rho], dev(dz=dz), zx_s.at[e, part, way])

            to_right, to_left = go(0, 7, 1), go(1, 1, 7)
            cond_sent.append((zl < 3, to_right))
            cond_sent.append((zl > 0, to_left))
            pl.when(zl < 3)(to_right.start)
            pl.when(zl > 0)(to_left.start)
        for part in range(2):
            theirs = (xo, do)[part].at[e]
            at = jnp.where(zl == 0, PLACE[1], jnp.where(zl == 1, PLACE[2], jnp.where(zl == 2, PLACE[6], PLACE[7])))
            hop = jnp.where(zl < 2, 7 - zl, 4 - zl)
            start(z_copy(e, part, theirs, at, dev(dz=hop), zo_s.at[e, part]))

    def is_right(rho):
        return zl >= 6 - rho

    def z_pass(e, rho):
        at = PLACE[rho]
        goes_right = is_right(rho)
        forward = jnp.where(goes_right, zl < 3, zl > 0)
        there = jnp.where(goes_right, PLACE[rho - 1], PLACE[(rho + 1) % 8])
        to = dev(dz=jnp.where(goes_right, 1, 7))
        for part in range(2):
            here = (xs, ds)[part].at[e, place(at)]
            z_copy(e, part, here, at, to, zf_s.at[e, part, at]).wait_recv()
            on = z_copy(e, part, here, there, to, zf_s.at[e, part, at])
            cond_sent.append((forward, on))
            pl.when(forward)(on.start)

    ones = jnp.ones((8, HID), F32)

    def compute(e, g):
        at = pl.ds(g * 2 * ROWS, 2 * ROWS)
        dtacc[...] = jnp.zeros_like(dtacc)
        gacc[...] = jnp.zeros_like(gacc)

        def shard(j, _):
            w_in = wi[e, j]
            pre = dot(xs[e, at, :], w_in)
            up = dot_nt(ds[e, at, :], wo[e, j])
            sq = pre * pre
            s = jnp.tanh(GELU_SCALE * (pre + GELU_CUBIC * sq * pre))
            half = 0.5 * (1.0 + s)
            a = (pre * half).astype(BF)
            slope = half + 0.5 * pre * (1.0 - s * s) * GELU_SCALE * (1.0 + 3.0 * GELU_CUBIC * sq)
            d = (up * slope).astype(BF)
            act[j, at, :] = a
            dpre[j, at, :] = d
            gacc[...] += a.astype(F32) * up
            dtacc[...] += dot_nt(d, w_in)
            return 0

        lax.fori_loop(0, 4, shard, 0)
        dt[e, at, :] = dtacc[...].astype(BF)
        for k in range(2):
            sums = lax.dot_general(
                ones, gacc[k * ROWS : (k + 1) * ROWS, :], (((1,), (1,)), ((), ())),
                precision=lax.Precision.HIGHEST, preferred_element_type=F32,
            )
            gp[2 * g + k, e * 8 : e * 8 + 8, 0:ROWS] = sums

    def y_scatter(e, kind):
        src = {
            "i_2": (dwi.at[e, 2], yri.at[e], right, 0),
            "o_2": (dwo.at[e, 2], yro.at[e], left, 1),
            "o_1": (dwo.at[e, 1], fin_lo.at[e], right, 2),
            "i_3": (dwi.at[e, 3], fin_ri.at[e], left, 3),
            "i_1": (dwi.at[e, 1], fin_li.at[e], right, 4),
            "o_3": (dwo.at[e, 3], fin_ro.at[e], left, 5),
        }[kind]
        return remote(src[0], src[1], yb_s.at[e, src[3]], yb_r.at[e, src[3]], src[2])

    def weight_grads(e):
        def part_in(j):
            return lambda t: dot_tn(xs[e, :, pl.ds(pl.multiple_of(t * 256, 256), 256)], dpre[j])

        def part_out(j):
            return lambda t: dot_tn(act[j], ds[e, :, pl.ds(pl.multiple_of(t * 256, 256), 256)])

        for j in (2, 1, 3, 0):

            def tile(t, _):
                cols = pl.ds(pl.multiple_of(t * 256, 256), 256)
                g_in, g_out = part_in(j)(t), part_out(j)(t)
                if j:
                    dwi[e, j, cols, :] = g_in.astype(BF)
                    dwo[e, j, :, cols] = g_out.astype(BF)
                else:
                    gwin_o[e, cols, :] = g_in
                    gwout_o[e, :, cols] = g_out
                return 0

            lax.fori_loop(0, 4, tile, 0)
            for kind in {2: ("i_2", "o_2"), 1: ("o_1",), 3: ("i_3",), 0: ()}[j]:
                start(y_scatter(e, kind))

    def y_relay(e):
        y_scatter(e, "i_2").wait_recv()
        dwi[e, 1] = (dwi[e, 1].astype(F32) + yri[e].astype(F32)).astype(BF)
        start(y_scatter(e, "i_1"))
        y_scatter(e, "o_2").wait_recv()
        dwo[e, 3] = (dwo[e, 3].astype(F32) + yro[e].astype(F32)).astype(BF)
        start(y_scatter(e, "o_3"))

    def y_final(e):
        for kind in ("o_1", "i_3", "i_1", "o_3"):
            y_scatter(e, kind).wait_recv()
        gwin_o[e] = gwin_o[e] + fin_li[e].astype(F32) + fin_ri[e].astype(F32)
        gwout_o[e] = gwout_o[e] + fin_lo[e].astype(F32) + fin_ro[e].astype(F32)

    def z_back(e, rho):
        at = place(PLACE[rho])
        goes_right = is_right(rho)
        incoming = jnp.where(goes_right, zl < 3, zl > 0)
        first = jnp.where(goes_right, zl == 0, zl == 3)
        slot = jnp.where(first, 9, jnp.where(goes_right, rho + 1, rho - 1))
        hop = jnp.where(first, rho, jnp.where(goes_right, 7, 1))
        here = dt.at[e, at]

        @pl.when(incoming)
        def _():
            remote(here, rb.at[e, rho], zb_s.at[e, rho], zb_r.at[e, rho], dev(dz=1)).wait_recv()
            dt[e, at, :] = (dt[e, at, :].astype(F32) + rb[e, rho].astype(F32)).astype(BF)

        start(remote(here, rb.at[e, slot], zb_s.at[e, rho], zb_r.at[e, slot], dev(dz=hop)))

    def z_home(e):
        total = dt[e, 0:ROWS, :].astype(F32)
        dtacc[0:ROWS, :] = total
        here = dt.at[e, place(0)]
        for cond, slot in ((zl < 3, 8), (zl > 0, 0)):

            @pl.when(cond)
            def _(slot=slot):
                remote(here, rb.at[e, slot], zb_s.at[e, 0], zb_r.at[e, slot], dev(dz=1)).wait_recv()
                dtacc[0:ROWS, :] += rb[e, slot].astype(F32)

        pack[e * ROWS : (e + 1) * ROWS, :] = dtacc[0:ROWS, :].astype(BF)
        remote(here, rb.at[e, 9], zb_s.at[e, 0], zb_r.at[e, 9], dev(dz=1)).wait_recv()
        pack[(2 + e) * ROWS : (3 + e) * ROWS, :] = rb[e, 9]

    def gate_copy(rho):
        return remote(gp.at[PLACE[rho]], gr.at[8 - rho], gt_s.at[rho], gt_r.at[8 - rho], dev(dz=rho))

    def back(rhos, e):
        for rho in rhos:
            z_back(e, rho)

    def z_passes(e, rhos):
        for rho in rhos:
            z_pass(e, rho)

    arrive(0)
    z_own(0)
    y_forward(0)
    y_own(1)
    z_passes(0, (1, 7))
    arrive(1)
    z_passes(0, (2, 6))
    for copy in local:
        copy.wait()
    y_rest(0)
    compute(0, 0)
    z_passes(0, (3, 5, 4))
    z_own(1)
    compute(0, 1)
    y_forward(1)
    compute(0, 2)
    compute(0, 3)
    z_passes(1, (1, 7))
    weight_grads(0)
    back((4, 5, 3), 0)
    z_passes(1, (2, 6))
    back((6, 2), 0)
    y_rest(1)
    compute(1, 0)
    y_relay(0)
    z_passes(1, (3, 5, 4))
    compute(1, 1)
    back((7, 1), 0)
    compute(1, 2)
    compute(1, 3)
    for rho in ORDER:
        start(gate_copy(rho))
    back((4, 5, 3), 1)
    weight_grads(1)
    z_home(0)
    back((6, 2, 7, 1), 1)
    y_final(0)
    z_home(1)

    own_sum, other_sum = gp[0], jnp.zeros((16, 128), F32)
    for rho in range(1, 8):
        gate_copy(8 - rho).wait_recv()
        near = jnp.where(rho < 4, rho <= 3 - zl, rho >= 8 - zl)
        value = gr[rho]
        own_sum += jnp.where(near, value, 0.0)
        other_sum += jnp.where(near, 0.0, value)
    line = iota((16, 128), 0)
    rows = jnp.zeros((16, 128), F32)
    for at, value in enumerate((own_sum[0:1], own_sum[8:9], other_sum[0:1], other_sum[8:9])):
        high = value.astype(BF).astype(F32)
        rows = jnp.where(line == at, high, jnp.where(line == at + 4, value - high, rows))
    pack[320:336, :] = jnp.zeros((16, D), BF)
    pack[320:336, 0:128] = rows.astype(BF)

    o, i = iota((8 * RET, 336), 0), iota((8 * RET, 336), 1)
    m, w = o // RET, o - (o // RET) * RET
    q = w // 10
    source = jnp.where(w < 40, q * ROWS + m * 10 + (w - q * 10), 320 + w - 40)
    chosen = (source == i).astype(F32).astype(BF)
    rets[...] = dot(chosen, pack[...]).astype(BF)

    def ret_copy(k, j):
        m = k * 2 + j
        n = (4 - k) % 4 * 2 + j
        return remote(
            rets.at[pl.ds(m * RET, RET)], retr.at[pl.ds(n * RET, RET)], rt_s.at[m], rt_r.at[n], dev(dx=k, dc=j)
        )

    peers = [(k, j) for k in (2, 1, 3, 0) for j in range(2) if k or j]
    for k, j in peers:
        start(ret_copy(k, j))
    retr[0:RET, :] = rets[0:RET, :]
    y_relay(1)
    for k, j in peers:
        ret_copy(k, j).wait_recv()
    line = iota((8 * RET, TOK), 0)
    both = (line == home[0][0]) | (line == home[1][0])
    gtok_o[...] = dot_tn(both.astype(F32).astype(BF), retr[...]).astype(BF)
    for k in range(2):
        gate_row, lane = home[k][1], home[k][2]
        rows_of = ((line == gate_row) | (line == gate_row + 4)).astype(F32).astype(BF)
        found = dot_tn(retr[:, 0:128], rows_of)
        value = jnp.sum(jnp.where(iota((128, TOK), 0) == lane, found, 0.0), axis=0, keepdims=True)
        ggate_o[k : k + 1, :] = value / meta[2 + k : 3 + k, :]
    y_final(1)
    for copy in sent:
        copy.wait_send()
    for cond, copy in cond_sent:
        pl.when(cond)(copy.wait_send)


def per_device(tokens, grad_out, expert_ids, gate_values, weight_in, weight_out):
    ids, gates = expert_ids.T.astype(F32), gate_values.T.astype(F32)
    meta = jnp.concatenate([ids, gates, jnp.zeros((4, TOK), F32)], axis=0)
    v, dma = pltpu.VMEM, pltpu.SemaphoreType.DMA
    scratch = [
        v((4 * TOK, D), BF), v((8, TOK), F32), v((2, 320, D), BF), v((2, 320, D), BF),
        v((2, 640, D), BF), v((2, 640, D), BF), v((2, ROWS, D), BF), v((2, ROWS, D), BF),
        v((2, 4, D, HID), BF), v((2, 4, HID, D), BF), v((4, 640, HID), BF), v((4, 640, HID), BF),
        v((2 * ROWS, D), F32), v((2 * ROWS, HID), F32), v((2, 640, D), BF), v((2, 10, ROWS, D), BF),
        v((8, 16, 128), F32), v((8, 16, 128), F32),
        v((2, 4, D, HID), BF), v((2, 4, HID, D), BF), v((2, D, HID), BF), v((2, HID, D), BF),
        v((2, D, HID), BF), v((2, HID, D), BF), v((2, D, HID), BF), v((2, HID, D), BF),
        v((336, D), BF), v((8 * RET, D), BF), v((8 * RET, D), BF),
        dma((3,)), dma((3,)), dma((2, 2)), dma((2, 4)), dma((2, 4)),
        dma((2, 2, 2)), dma((2, 2, 8)), dma((2, 2, 8)), dma((2, 2)), dma((2, 6)), dma((2, 6)),
        dma((2, 8)), dma((2, 10)), dma((8,)), dma((8,)), dma((2, 6)), dma((2, 6)), dma((8,)), dma((8,)),
    ]
    vm, hbm = pl.BlockSpec(memory_space=pltpu.VMEM), pl.BlockSpec(memory_space=pl.ANY)
    gtok, ggate, gwin, gwout = pl.pallas_call(
        kernel,
        out_shape=[
            jax.ShapeDtypeStruct((TOK, D), BF),
            jax.ShapeDtypeStruct((2, TOK), F32),
            jax.ShapeDtypeStruct((2, D, HID), F32),
            jax.ShapeDtypeStruct((2, HID, D), F32),
        ],
        in_specs=[vm, vm, vm, hbm, hbm],
        out_specs=[vm, vm, vm, vm],
        scratch_shapes=scratch,
        compiler_params=pltpu.CompilerParams(
            collective_id=0, has_side_effects=True, vmem_limit_bytes=62 * 2**20
        ),
        name="moe_backward",
    )(tokens, grad_out, meta, weight_in, weight_out)
    return gtok, ggate.T, gwin, gwout


def solution(mesh):
    placed = (
        P(("dp", "expert"), None),
        P(("dp", "expert"), None),
        P(("dp", "expert"), None),
        P(("dp", "expert"), None),
        P("expert", None, "dp"),
        P("expert", "dp", None),
    )
    return jax.shard_map(
        per_device,
        mesh=mesh,
        in_specs=placed,
        out_specs=(
            P(("dp", "expert"), None),
            P(("dp", "expert"), None),
            P("expert", None, "dp"),
            P("expert", "dp", None),
        ),
        check_vma=False,
    )
```

time: 571 us -> 198 us (0.35)
  waiting for transfers between devices: 275 us -> 0 us
  Pallas kernels: 0 us -> 187 us
  blocking collectives: 184 us -> 0 us
  matrix products: 56.4 us -> 0 us
  starting transfers between devices: 26 us -> 0 us
  between operations: 14 us -> 0.65 us
    pallas_call x0 -> x1, Pallas kernels: none -> 187 us  [per_device(): pl.pallas_call(kernel, out_shape=[jax.ShapeDtypeStruct((TOK, D), BF), jax...]
    all_gather x1 -> x0, blocking collectives: 116 us -> none  [per_device(): lax.all_gather(arrived[2], 'dp', axis=2, tiled=True)]
    reduce_scatter x1 -> x0, waiting for transfers between devices: 113 us -> none  [per_device(): lax.psum_scatter(jnp.einsum('lrf,ldf->rld', hidden_store, weight_in, pref...]
    all_gather x2 -> x0, waiting for transfers between devices: 99.1 us -> none  [the longest x1 99.1 us: per_device(): lax.all_gather(arrived[1], 'dp', axis=2, tiled=True)]
    all_to_all x3 -> x0, blocking collectives: 67.3 us -> none  [the longest x1 29.1 us: per_device(): lax.all_to_all(slot_x.reshape(slot_shape), 'expert', split_axis=0, concat...]
    unnamed x5 -> x0, waiting for transfers between devices: 63 us -> none
    dot_general x10 -> x0, matrix products: 56.4 us -> none  [the longest x1 12.8 us: expert_piece(): jnp.einsum('lrd,ldf->lrf', routed_x, weight_in, preferred_element_type=jn...]
    all_to_all x2 -> x0, starting transfers between devices: 25.7 us -> none  [the longest x1 18.3 us: per_device(): lax.all_to_all(gate_mine.reshape(expert_count, capacity, local_experts).a...]
  transfers between devices with their start and end apart: 6 -> 0, of which waited for: 3 -> 0; matrix products, arithmetic and copies ran while one was open for 9% -> 0% of each run, Pallas kernels for 0% -> 0%
where the time goes in v1:
time: 198 us; the launch traced here: 197 us
  Pallas kernels  187 us (94%)
  local copies, waits for them, and re-layouts  7.46 us (4%)
  other arithmetic  2 us (1%)
    pallas_call x1, Pallas kernels, per_device(): pl.pallas_call(kernel, out_shape=[jax.ShapeDtypeStruct((TOK, D), BF), jax...  187 us
    unnamed x6, local copies, waits for them, and re-layouts  7.38 us

profile of v1, /device:TPU:1, one launch (start us, length us, event | category | flops | bytes accessed | tf_op | source)
XLA Modules:
  0.0 197.2 jit_solution(12660801577135061094)
XLA Ops:
  0.6 0.1 pad.2.clone
  0.7 0.7 convert_bitcast_fusion.1
  1.4 0.7 convert_bitcast_fusion
  2.1 0.7 maximum_maximum_fusion.meta
  2.7 187.1 %moe_backward.1 = (bf16[128,1024]{1,0:T(8,128)(2,1)}, f32[2,128]{1,0:T(2,128)}, f32[2,1024,256]{2,1,0:T(8,128)}, f32[2,256,1024]{2,1,0:T(8,128)}) custom-call(bf16[128,1024]{1,0:T(8,128)(2,1)} %tok.1, bf16[128,1024]{1,0:T(8,128)(2,1)} %gout.1, f32[8,128]{1,0:T(8,128)} %maximum_maximum_fusion.meta, bf16[2,1024,256]{2,1,0:T(8,128)(2,1)} %win.1, ...), custom_call_target="tpu_custom_call" | custom-call | tf_op jit(solution)/shard_map/moe_backward/pallas_call | solution.py:476
  189.8 1.7 copy.14
  191.5 1.2 copy.15
  192.7 0.0 copy-start
  192.7 3.2 %copy.16 = f32[2,1024,256]{2,1,0:T(8,128)} copy(f32[2,1024,256]{2,1,0:T(8,128)} %get-tuple-element.18) | data formatting | bytes 4194304
  195.9 0.0 copy-done
  195.9 1.3 copy.17
  (1 shorter events, 0.0 us)
Async XLA Ops:
  192.7 3.2 %copy-start = (f32[2,256,1024]{2,1,0:T(8,128)S(1)}, f32[2,256,1024]{2,1,0:T(8,128)}, u32[]{:S(2)}) copy-start(f32[2,256,1024]{2,1,0:T(8,128)} %get-tuple-element.19) | copy-start | bytes 6291460

commit v2 on v1

v2 whole, which is shorter than its diff:
```python
import functools

import jax
import jax.numpy as jnp
from jax import lax
from jax.experimental import pallas as pl
from jax.experimental.pallas import tpu as pltpu
from jax.sharding import PartitionSpec as P

MESH = pl.DeviceIdType.MESH
BF, F32 = jnp.bfloat16, jnp.float32
GELU_SCALE = 0.7978845608028654
GELU_CUBIC = 0.044715

D = 1024
HID = 256
TOK = 128
CAP = 10
ROWS = 8 * CAP
RET = 32

PLACE = {7: 0, 1: 1, 6: 2, 2: 3, 5: 4, 3: 5, 4: 6, 0: 7}
OWN = slice(PLACE[0] * ROWS, PLACE[0] * ROWS + ROWS)
ORDER = (1, 7, 2, 6, 3, 5, 4)


def dot(a, b):
    return lax.dot_general(a, b, (((1,), (0,)), ((), ())), preferred_element_type=F32)


def dot_nt(a, b):
    return lax.dot_general(a, b, (((1,), (1,)), ((), ())), preferred_element_type=F32)


def dot_tn(a, b):
    return lax.dot_general(a, b, (((0,), (0,)), ((), ())), preferred_element_type=F32)


def iota(shape, dim):
    return lax.broadcasted_iota(jnp.int32, shape, dim)


def kernel(
    tok, gout, ids, gate, win, wout,
    gtok_o, ggate_o, own_io, own_oo, fin_li, fin_lo, fin_ri, fin_ro,
    raw, meta, meta_far, ms, mr, xs, ds, xo, do,
    wi, wo, act, dpre, dtacc, gacc, dt, rb, gp, gr,
    dwi, dwo, yri, yro, own_i, own_o,
    pack, rets, retr,
    core_s, core_r, loc_s, xs_s, xs_r, zx_s, zx_r, zf_s, zo_s, ya_s, ya_r,
    zb_s, zb_r, gt_s, gt_r, yb_s, yb_r, rt_s, rt_r, out_s,
):
    dp, ex = lax.axis_index("dp"), lax.axis_index("expert")
    zl, y = dp // 4, dp % 4
    zh, x, c = ex // 8, (ex // 2) % 4, ex % 2
    z = zh * 4 + zl

    def dev(dz=0, dy=0, dx=0, dc=0):
        zz, yy, xx, cc = (z + dz + 8) % 8, (y + dy + 4) % 4, (x + dx + 4) % 4, (c + dc) % 2
        return ((zz % 4) * 4 + yy, (zz // 4) * 8 + xx * 2 + cc)

    def remote(src, dst, send, recv, to):
        return pltpu.make_async_remote_copy(
            src_ref=src, dst_ref=dst, send_sem=send, recv_sem=recv, device_id=to, device_id_type=MESH
        )

    barrier = pltpu.get_barrier_semaphore()
    partners = [dev(dz=k) for k in range(1, 8)] + [dev(dy=1), dev(dy=3)]
    partners += [dev(dx=k, dc=j) for k in range(4) for j in range(2) if k or j]
    for to in partners:
        pl.semaphore_signal(barrier, inc=1, device_id=to, device_id_type=MESH)
    pl.semaphore_wait(barrier, len(partners))

    sent = []

    def start(copy):
        copy.start()
        sent.append(copy)
        return copy

    right, left = dev(dy=1), dev(dy=3)

    def y_gather(e, kind):
        src = {
            "i_r": (win.at[e], wi.at[e, 3], right, 0),
            "o_r": (wout.at[e], wo.at[e, 3], right, 1),
            "i_l": (win.at[e], wi.at[e, 1], left, 2),
            "o_l": (wout.at[e], wo.at[e, 1], left, 3),
            "i_f": (wi.at[e, 3], wi.at[e, 2], right, 4),
            "o_f": (wo.at[e, 1], wo.at[e, 2], left, 5),
        }[kind]
        return remote(src[0], src[1], ya_s.at[e, src[3]], ya_r.at[e, src[3]], src[2])

    def y_own(e, kinds):
        for kind in kinds:
            start(y_gather(e, kind))

    def y_forward(e):
        y_gather(e, "i_r").wait_recv()
        start(y_gather(e, "i_f"))
        y_gather(e, "o_l").wait_recv()
        start(y_gather(e, "o_f"))

    def y_rest(e):
        for kind in ("o_r", "i_l", "i_f", "o_f"):
            y_gather(e, kind).wait_recv()

    meta[...] = jnp.concatenate([ids[...].astype(F32), gate[...].astype(F32), jnp.zeros((4, TOK), F32)], axis=0)
    core = dev(dc=1)
    swaps = [
        remote(meta, meta_far, core_s.at[0], core_r.at[0], core),
        remote(tok, raw.at[pl.ds(TOK, TOK)], core_s.at[1], core_r.at[1], core),
        remote(gout, raw.at[pl.ds(3 * TOK, TOK)], core_s.at[2], core_r.at[2], core),
    ]
    for copy in swaps:
        start(copy)
    y_own(0, ("i_r", "o_l"))
    local = []
    for e in range(2):
        local.append(pltpu.make_async_copy(win.at[e], wi.at[e, 0], loc_s.at[e, 0]))
        local.append(pltpu.make_async_copy(wout.at[e], wo.at[e, 0], loc_s.at[e, 1]))
    for copy in local:
        copy.start()

    raw[0:TOK, :] = tok[...]
    raw[2 * TOK : 3 * TOK, :] = gout[...]
    before = (iota((TOK, TOK), 0) < iota((TOK, TOK), 1)).astype(F32).astype(BF)

    def ranks(ids0, ids1, wanted):
        hit0, hit1 = ids0 == wanted, ids1 == wanted
        hit = jnp.where(hit0 | hit1, 1.0, 0.0)
        return hit, dot(hit.astype(BF), before), hit0, hit1

    swaps[0].wait_recv()
    k = iota((16, TOK), 0)
    k_x, k_zone, k_e = (x + (k >> 2)) & 3, (zh + (k & 1)) & 1, (k >> 1) & 1
    wanted = ((k_zone * 8 + k_x * 2 + c) * 2 + k_e).astype(F32)
    codes, gates = [], []
    for side, m in enumerate((meta, meta_far)):
        hit, rank, h0, h1 = ranks(m[0:1, :], m[1:2, :], wanted)
        codes.append(jnp.where(hit > 0.0, rank + side * CAP, -1.0))
        gates.append(jnp.where(h0, m[2:3, :], 0.0) + jnp.where(h1, m[3:4, :], 0.0))
    code = jnp.concatenate(codes, axis=1).astype(jnp.int32)
    weight = jnp.concatenate(gates, axis=1)

    def x_send(part, k):
        return remote(
            ms.at[part, pl.ds(k * 80, 80)], mr.at[part, pl.ds((4 - k) % 4 * 80, 80)],
            xs_s.at[part, k], xs_r.at[part, k], dev(dx=k),
        )

    def dispatch(part):
        blocks = []
        for k in range(16):
            same = iota((20, 2 * TOK), 0) == code[k : k + 1, :]
            blocks.append(jnp.where(same, weight[k : k + 1, :] if part else 1.0, 0.0))
        spread = jnp.concatenate(blocks, axis=0).astype(BF)
        rows = dot(spread, raw[part * 2 * TOK : (part + 1) * 2 * TOK, :]).astype(BF)
        ms[part] = rows
        for k in (1, 3, 2):
            start(x_send(part, k))
        mr[part, 0:80, :] = rows[0:80, :]

    swaps[1].wait_recv()
    dispatch(0)
    swaps[2].wait_recv()
    dispatch(1)
    y_own(0, ("o_r", "i_l"))
    gp[...] = jnp.zeros_like(gp)

    number = iota((32, TOK), 0)
    own0, own1 = meta[0:1, :], meta[1:2, :]
    _, own_rank, hit0, hit1 = ranks(own0, own1, number.astype(F32))
    num_ex = number >> 1
    xr = (((num_ex >> 1) & 3) - x + 4) & 3
    cr = (num_ex + c) & 1
    zr = ((num_ex >> 3) + zh) & 1
    message = (number & 1) * (8 * RET) + (xr * 2 + cr) * RET
    row_code = (message + zr * 10).astype(F32) + own_rank
    gate_code = (message + 20 + zr).astype(F32)
    lane_code = (((4 - xr) & 3) * 20 + cr * 10).astype(F32) + own_rank

    def pick(hit, table):
        return jnp.sum(jnp.where(hit, table, 0.0), axis=0, keepdims=True).astype(jnp.int32)

    home = [[pick(hit, t) for t in (row_code, gate_code, lane_code)] for hit in (hit0, hit1)]

    o, i = iota((320, 320), 0), iota((320, 320), 1)
    oa, ia = o // 20, i // 20
    unpack = ((o - oa * 20 == i - ia * 20) & ((oa & 3) == (ia >> 2)) & ((oa >> 2) == (ia & 3)))
    unpack = unpack.astype(F32).astype(BF)

    def arrive(part):
        for k in (1, 3, 2):
            x_send(part, k).wait_recv()
        rows = dot(unpack, mr[part]).astype(BF)
        mine, theirs = (xs, ds)[part], (xo, do)[part]
        for e in range(2):
            mine[e, OWN, :] = rows[e * 160 : e * 160 + 80, :]
            theirs[e] = rows[e * 160 + 80 : e * 160 + 160, :]

    def place(at):
        return pl.ds(at * ROWS, ROWS)

    def z_copy(e, part, src, at, to, send):
        where = (xs, ds)[part]
        return remote(src, where.at[e, place(at)], send, zx_r.at[e, part, at], to)

    cond_sent = []

    def z_own(e, busy, parts=(0, 1)):
        def send(cond, copy):
            cond_sent.append((cond, copy))
            pl.when(cond)(copy.start)

        for part in parts:
            mine, theirs = (xs, ds)[part].at[e, place(PLACE[0])], (xo, do)[part].at[e]

            def go(way, rho, dz):
                return z_copy(e, part, mine, PLACE[rho], dev(dz=dz), zx_s.at[e, part, way])

            inner = (zl == 1) | (zl == 2)
            at = jnp.where(zl == 0, PLACE[1], jnp.where(zl == 1, PLACE[2], jnp.where(zl == 2, PLACE[6], PLACE[7])))
            hop = jnp.where(zl < 2, 7 - zl, 4 - zl)
            send(zl == 2 if busy else zl < 2, go(0, 7, 1))
            send(zl == 1 if busy else zl > 1, go(1, 1, 7))
            send(inner if busy else ~inner, z_copy(e, part, theirs, at, dev(dz=hop), zo_s.at[e, part]))

    def is_right(rho):
        return zl >= 6 - rho

    def z_waits(e, rhos, parts=(0, 1)):
        for rho in rhos:
            at = PLACE[rho]
            for part in parts:
                here = (xs, ds)[part].at[e, place(at)]
                z_copy(e, part, here, at, dev(dz=1), zf_s.at[e, part, at]).wait_recv()

    def z_on(e, rho, part):
        at = PLACE[rho]
        goes_right = is_right(rho)
        forward = jnp.where(goes_right, zl < 3, zl > 0)
        there = jnp.where(goes_right, PLACE[rho - 1], PLACE[(rho + 1) % 8])
        to = dev(dz=jnp.where(goes_right, 1, 7))
        return forward, z_copy(e, part, (xs, ds)[part].at[e, place(at)], there, to, zf_s.at[e, part, at])

    def z_passes(e, rhos, parts=(0, 1)):
        for rho in rhos:
            for part in parts:
                z_waits(e, (rho,), (part,))
                forward, on = z_on(e, rho, part)
                pl.when(forward)(on.start)

    ones = jnp.ones((8, HID), F32)

    def compute(e, g):
        at = pl.ds(pl.multiple_of(g * 2 * ROWS, 2 * ROWS), 2 * ROWS)
        dtacc[...] = jnp.zeros_like(dtacc)
        gacc[...] = jnp.zeros_like(gacc)

        def shard(j, _):
            w_in = wi[e, j]
            pre = dot(xs[e, at, :], w_in)
            up = dot_nt(ds[e, at, :], wo[e, j])
            sq = pre * pre
            s = jnp.tanh(GELU_SCALE * (pre + GELU_CUBIC * sq * pre))
            half = 0.5 * (1.0 + s)
            a = (pre * half).astype(BF)
            slope = half + 0.5 * pre * (1.0 - s * s) * GELU_SCALE * (1.0 + 3.0 * GELU_CUBIC * sq)
            d = (up * slope).astype(BF)
            act[j, at, :] = a
            dpre[j, at, :] = d
            gacc[...] += a.astype(F32) * up
            dtacc[...] += dot_nt(d, w_in)
            return 0

        lax.fori_loop(0, 4, shard, 0)
        dt[e, at, :] = dtacc[...].astype(BF)
        for k in range(2):
            sums = lax.dot_general(
                ones, gacc[k * ROWS : (k + 1) * ROWS, :], (((1,), (1,)), ((), ())),
                precision=lax.Precision.HIGHEST, preferred_element_type=F32,
            )
            gp[e, 2 * g + k, :, 0:ROWS] = sums

    def y_scatter(e, kind):
        src = {
            "i_2": (dwi.at[e, 2], yri.at[e], right, 0),
            "o_2": (dwo.at[e, 2], yro.at[e], left, 1),
            "o_1": (dwo.at[e, 1], fin_lo.at[e], right, 2),
            "i_3": (dwi.at[e, 3], fin_ri.at[e], left, 3),
            "i_1": (dwi.at[e, 1], fin_li.at[e], right, 4),
            "o_3": (dwo.at[e, 3], fin_ro.at[e], left, 5),
        }[kind]
        return remote(src[0], src[1], yb_s.at[e, src[3]], yb_r.at[e, src[3]], src[2])

    def weight_grads(e, j):
        def tile(t, _):
            cols = pl.ds(pl.multiple_of(t * 256, 256), 256)
            g_in, g_out = dot_tn(xs[e, :, cols], dpre[j]), dot_tn(act[j], ds[e, :, cols])
            if j:
                dwi[e, j, cols, :] = g_in.astype(BF)
                dwo[e, j, :, cols] = g_out.astype(BF)
            else:
                own_i[e, cols, :] = g_in
                own_o[e, :, cols] = g_out
            return 0

        lax.fori_loop(0, 4, tile, 0)
        for kind in {2: ("i_2", "o_2"), 1: ("o_1",), 3: ("i_3",), 0: ()}[j]:
            start(y_scatter(e, kind))
        if j == 0:
            for k, (a, b) in enumerate(((own_i, own_io), (own_o, own_oo))):
                copy = pltpu.make_async_copy(a.at[e], b.at[e], out_s.at[e, k])
                copy.start()
                outs.append(copy)

    outs = []

    def y_relay(e):
        y_scatter(e, "i_2").wait_recv()
        dwi[e, 1] = (dwi[e, 1].astype(F32) + yri[e].astype(F32)).astype(BF)
        start(y_scatter(e, "i_1"))
        y_scatter(e, "o_2").wait_recv()
        dwo[e, 3] = (dwo[e, 3].astype(F32) + yro[e].astype(F32)).astype(BF)
        start(y_scatter(e, "o_3"))

    def y_final(e):
        for kind in ("o_1", "i_3", "i_1", "o_3"):
            y_scatter(e, kind).wait_recv()

    def z_back(e, rho):
        spot = jnp.where(rho >= 5, 14 - 2 * rho, jnp.where(rho == 4, 6, 2 * rho - 1))
        at = pl.ds(pl.multiple_of(spot * ROWS, ROWS), ROWS)
        goes_right = is_right(rho)
        incoming = jnp.where(goes_right, zl < 3, zl > 0)
        first = jnp.where(goes_right, zl == 0, zl == 3)
        slot = jnp.where(first, 9, jnp.where(goes_right, rho + 1, rho - 1))
        hop = jnp.where(first, rho, jnp.where(goes_right, 7, 1))
        here = dt.at[e, at]

        @pl.when(incoming)
        def _():
            remote(here, rb.at[e, rho], zb_s.at[e, rho], zb_r.at[e, rho], dev(dz=1)).wait_recv()
            dt[e, at, :] = (dt[e, at, :].astype(F32) + rb[e, rho].astype(F32)).astype(BF)

        remote(here, rb.at[e, slot], zb_s.at[e, rho], zb_r.at[e, slot], dev(dz=hop)).start()

    edge = (zl == 0) | (zl == 3)

    def back_edge(e, pairs):
        for at_0, at_3 in pairs:
            pl.when(edge)(lambda: z_back(e, jnp.where(zl == 0, at_0, at_3)))

    def back_inner(e, pairs):
        for at_1, at_2 in pairs:
            pl.when(~edge)(lambda: z_back(e, jnp.where(zl == 1, at_1, at_2)))

    inner_first = ((1, 7), (2, 6), (7, 5), (6, 1))
    inner_last = ((3, 4), (4, 2), (5, 3))
    edge_last = ((7, 1), (6, 2))

    def z_home(e):
        own = dt.at[e, place(PLACE[0])]
        dtacc[0:ROWS, :] = dt[e, OWN, :].astype(F32)
        for cond, slot in ((zl < 3, 8), (zl > 0, 0)):

            @pl.when(cond)
            def _(slot=slot):
                remote(own, rb.at[e, slot], zb_s.at[e, 0], zb_r.at[e, slot], dev(dz=1)).wait_recv()
                dtacc[0:ROWS, :] += rb[e, slot].astype(F32)

        pack[0:ROWS, :] = dtacc[0:ROWS, :].astype(BF)
        remote(own, rb.at[e, 9], zb_s.at[e, 0], zb_r.at[e, 9], dev(dz=1)).wait_recv()
        pack[ROWS : 2 * ROWS, :] = rb[e, 9]

    def gate_copy(e, rho):
        return remote(
            gp.at[e, PLACE[rho]], gr.at[e, 8 - rho], gt_s.at[e, rho], gt_r.at[e, 8 - rho], dev(dz=rho)
        )

    def gates_out(e):
        for rho in ORDER:
            start(gate_copy(e, rho))

    peers = [(k, j) for k in (2, 1, 3, 0) for j in range(2) if k or j]

    def ret_copy(e, k, j):
        m = k * 2 + j
        n = (4 - k) % 4 * 2 + j
        return remote(
            rets.at[e, pl.ds(m * RET, RET)], retr.at[pl.ds(e * 8 * RET + n * RET, RET)],
            rt_s.at[e, m], rt_r.at[e, n], dev(dx=k, dc=j),
        )

    def give_back(e):
        z_home(e)
        own_sum, other_sum = gp[e, PLACE[0]], jnp.zeros((8, 128), F32)
        for rho in range(1, 8):
            gate_copy(e, 8 - rho).wait_recv()
            near = jnp.where(rho < 4, rho <= 3 - zl, rho >= 8 - zl)
            value = gr[e, rho]
            own_sum += jnp.where(near, value, 0.0)
            other_sum += jnp.where(near, 0.0, value)
        line = iota((16, 128), 0)
        rows = jnp.zeros((16, 128), F32)
        for at, value in enumerate((own_sum[0:1], other_sum[0:1])):
            high = value.astype(BF).astype(F32)
            rows = jnp.where(line == at, high, jnp.where(line == at + 2, value - high, rows))
        pack[160:176, :] = jnp.zeros((16, D), BF)
        pack[160:176, 0:128] = rows.astype(BF)
        o, i = iota((8 * RET, 176), 0), iota((8 * RET, 176), 1)
        m, w = o >> 5, o & 31
        q = w // 10
        source = jnp.where(w < 20, q * ROWS + m * 10 + (w - q * 10), 160 + w - 20)
        chosen = (source == i).astype(F32).astype(BF)
        rets[e] = dot(chosen, pack[...]).astype(BF)
        for k, j in peers:
            start(ret_copy(e, k, j))
        retr[e * 8 * RET : e * 8 * RET + RET, :] = rets[e, 0:RET, :]

    def last_passes(e, between):
        if e == 0:
            pl.when(~edge)(lambda: z_passes(e, (3, 5, 4), (1,)))
            z_own(1, True)
        else:
            pl.when(~edge)(lambda: z_passes(e, (3, 5, 4)))
        pl.when(edge)(lambda: z_waits(e, (4,)))
        compute(e, 3)
        back_edge(e, ((4, 4),))
        between()
        pl.when(edge)(lambda: z_waits(e, (3, 5)))
        compute(e, 2)
        back_edge(e, ((3, 5), (5, 3)))

    arrive(0)
    z_own(0, True, (0,))
    z_own(0, False, (0,))
    z_passes(0, (1, 7), (0,))
    arrive(1)
    z_own(0, True, (1,))
    z_own(0, False, (1,))
    y_forward(0)
    z_passes(0, (2, 6), (0,))
    z_passes(0, (1, 7), (1,))
    y_own(1, ("i_r", "o_l"))
    pl.when(~edge)(lambda: z_passes(0, (3, 5, 4), (0,)))
    z_passes(0, (2, 6), (1,))
    z_own(1, False)
    y_own(1, ("o_r", "i_l"))
    for copy in local:
        copy.wait()
    y_rest(0)
    compute(0, 0)
    compute(0, 1)
    back_edge(0, ((1, 7), (2, 6)))
    last_passes(0, lambda: y_forward(1))
    weight_grads(0, 2)
    z_passes(1, (1, 7))
    gates_out(0)
    back_inner(0, inner_first)
    weight_grads(0, 1)
    weight_grads(0, 3)
    z_passes(1, (2, 6))
    weight_grads(0, 0)
    back_inner(0, inner_last)
    back_edge(0, edge_last)
    y_rest(1)
    compute(1, 0)
    y_relay(0)
    compute(1, 1)
    back_edge(1, ((1, 7), (2, 6)))
    last_passes(1, lambda: None)
    weight_grads(1, 2)
    back_inner(1, inner_first)
    gates_out(1)
    give_back(0)
    weight_grads(1, 1)
    weight_grads(1, 3)
    back_inner(1, inner_last)
    back_edge(1, edge_last)
    weight_grads(1, 0)
    y_final(0)
    give_back(1)
    y_relay(1)
    for e in range(2):
        for k, j in peers:
            ret_copy(e, k, j).wait_recv()
    line = iota((16 * RET, TOK), 0)
    both = (line == home[0][0]) | (line == home[1][0])
    gtok_o[...] = dot_tn(both.astype(F32).astype(BF), retr[...]).astype(BF)
    for k in range(2):
        gate_row, lane = home[k][1], home[k][2]
        rows_of = ((line == gate_row) | (line == gate_row + 2)).astype(F32).astype(BF)
        found = dot_tn(retr[:, 0:128], rows_of)
        value = jnp.sum(jnp.where(iota((128, TOK), 0) == lane, found, 0.0), axis=0, keepdims=True)
        ggate_o[k : k + 1, :] = value / meta[2 + k : 3 + k, :]
    y_final(1)
    for copy in sent:
        copy.wait_send()
    cond_sent += [z_on(e, rho, part) for e in range(2) for rho in ORDER for part in range(2)]
    for cond, copy in cond_sent:
        pl.when(cond)(copy.wait_send)
    for e in range(2):
        for rho in range(1, 8):
            remote(dt.at[e, place(0)], rb.at[e, rho], zb_s.at[e, rho], zb_r.at[e, rho], dev(dz=1)).wait_send()
    for copy in outs:
        copy.wait()


def per_device(tokens, grad_out, expert_ids, gate_values, weight_in, weight_out):
    v, dma = pltpu.VMEM, pltpu.SemaphoreType.DMA
    scratch = [
        v((4 * TOK, D), BF), v((8, TOK), F32), v((8, TOK), F32), v((2, 320, D), BF), v((2, 320, D), BF),
        v((2, 640, D), BF), v((2, 640, D), BF), v((2, ROWS, D), BF), v((2, ROWS, D), BF),
        v((2, 4, D, HID), BF), v((2, 4, HID, D), BF), v((4, 640, HID), BF), v((4, 640, HID), BF),
        v((2 * ROWS, D), F32), v((2 * ROWS, HID), F32), v((2, 640, D), BF), v((2, 10, ROWS, D), BF),
        v((2, 8, 8, 128), F32), v((2, 8, 8, 128), F32),
        v((2, 4, D, HID), BF), v((2, 4, HID, D), BF), v((2, D, HID), BF), v((2, HID, D), BF),
        v((2, D, HID), F32), v((2, HID, D), F32),
        v((176, D), BF), v((2, 8 * RET, D), BF), v((16 * RET, D), BF),
        dma((3,)), dma((3,)), dma((2, 2)), dma((2, 4)), dma((2, 4)),
        dma((2, 2, 2)), dma((2, 2, 8)), dma((2, 2, 8)), dma((2, 2)), dma((2, 6)), dma((2, 6)),
        dma((2, 8)), dma((2, 10)), dma((2, 8)), dma((2, 8)), dma((2, 6)), dma((2, 6)), dma((2, 8)), dma((2, 8)),
        dma((2, 2)),
    ]
    vm, hbm = pl.BlockSpec(memory_space=pltpu.VMEM), pl.BlockSpec(memory_space=pl.ANY)
    shapes = [((TOK, D), BF), ((2, TOK), F32), ((2, D, HID), F32), ((2, HID, D), F32)]
    shapes += [((2, D, HID), BF), ((2, HID, D), BF)] * 2
    gtok, ggate, own_i, own_o, left_i, left_o, right_i, right_o = pl.pallas_call(
        kernel,
        out_shape=[jax.ShapeDtypeStruct(*of) for of in shapes],
        in_specs=[vm, vm, vm, vm, hbm, hbm],
        out_specs=[vm, vm, hbm, hbm, hbm, hbm, hbm, hbm],
        scratch_shapes=scratch,
        compiler_params=pltpu.CompilerParams(
            collective_id=0, has_side_effects=True, vmem_limit_bytes=62 * 2**20
        ),
        name="moe_backward",
    )(tokens, grad_out, expert_ids.T, gate_values.T, weight_in, weight_out)
    gwin = own_i + left_i.astype(F32) + right_i.astype(F32)
    gwout = own_o + left_o.astype(F32) + right_o.astype(F32)
    return gtok, ggate.T, gwin, gwout


def solution(mesh):
    placed = (
        P(("dp", "expert"), None),
        P(("dp", "expert"), None),
        P(("dp", "expert"), None),
        P(("dp", "expert"), None),
        P("expert", None, "dp"),
        P("expert", "dp", None),
    )
    return jax.shard_map(
        per_device,
        mesh=mesh,
        in_specs=placed,
        out_specs=(
            P(("dp", "expert"), None),
            P(("dp", "expert"), None),
            P("expert", None, "dp"),
            P("expert", "dp", None),
        ),
        check_vma=False,
    )
```

time: 198 us -> 181 us (0.914)
  Pallas kernels: 187 us -> 171 us
  local copies, waits for them, and re-layouts: 7.46 us -> 1.29 us
  other arithmetic: 2 us -> 5.74 us
    pallas_call x1, Pallas kernels: 187 us -> 171 us  [per_device(): pl.pallas_call(kernel, out_shape=[jax.ShapeDtypeStruct(*of) for of in sha...]
    unnamed x6 -> x12, local copies, waits for them, and re-layouts: 7.38 us -> 1.29 us
    add x0 -> x2, other arithmetic: none -> 5.74 us  [the longest x1 3.93 us: per_device(): gwin = own_i + left_i.astype(F32) + right_i.astype(F32)]
where the time goes in v2:
time: 181 us; the launch traced here: 179 us
  Pallas kernels  171 us (94%)
  other arithmetic  5.74 us (3%)
    pallas_call x1, Pallas kernels, per_device(): pl.pallas_call(kernel, out_shape=[jax.ShapeDtypeStruct(*of) for of in sha...  171 us
    add x1, other arithmetic, per_device(): gwin = own_i + left_i.astype(F32) + right_i.astype(F32)  3.93 us

profile of v2, /device:TPU:1, one launch (start us, length us, event | category | flops | bytes accessed | tf_op | source)
XLA Modules:
  0.0 178.8 jit_solution(2955051324897391357)
XLA Ops:
  0.6 171.1 %moe_backward.1 = (bf16[128,1024]{1,0:T(8,128)(2,1)}, f32[2,128]{1,0:T(2,128)}, f32[2,1024,256]{2,1,0:T(8,128)}, f32[2,256,1024]{2,1,0:T(8,128)}, bf16[2,1024,25...) custom-call(bf16[128,1024]{1,0:T(8,128)(2,1)} %tok.1, ...), custom_call_target="tpu_custom_call" | custom-call | tf_op jit(solution)/shard_map/moe_backward/pallas_call | solution.py:530
  171.7 0.0 copy-start
  171.7 0.0 copy-start.1
  171.7 0.0 copy-start.2
  171.7 3.9 %convert_add_fusion.1 = f32[2,1024,256]{2,1,0:T(8,128)} fusion(bf16[2,1024,256]{2,1,0:T(8,128)(2,1)} %get-tuple-element.16, f32[2,1024,256]{2,1,0:T(8,128)} %get-tuple-element.14, bf16[2,1024,256]{2,1,0:T(8,128)(2,1)} %get-tuple-element.15), kind=kLoop, calls=%fused_computation.1 | loop fusion | flops 2097152 | bytes 6291456 | tf_op jit(solution)/shard_map/add | solution.py:541
  175.6 0.0 copy-done
  175.7 0.0 copy-done.1
  175.7 0.0 copy-done.2
  175.7 0.0 copy-start.3
  175.7 0.0 copy-start.4
  175.7 1.8 %convert_add_fusion = f32[2,256,1024]{2,1,0:T(8,128)} fusion(bf16[2,256,1024]{2,1,0:T(8,128)(2,1)S(1)} %copy-done.2, f32[2,256,1024]{2,1,0:T(8,128)S(1)} %copy-done, bf16[2,256,1024]{2,1,0:T(8,128)(2,1)S(1)} %copy-done.1), kind=kLoop, calls=%fused_computation | loop fusion | flops 2097152 | bytes 6291456 | tf_op jit(solution)/shard_map/add | solution.py:542
  177.5 0.0 copy-done.3
  177.5 0.7 copy.12
  178.2 0.0 copy-done.4
  178.2 0.6 copy.13
Async XLA Ops:
  171.7 4.0 %copy-start = (f32[2,256,1024]{2,1,0:T(8,128)S(1)}, f32[2,256,1024]{2,1,0:T(8,128)}, u32[]{:S(2)}) copy-start(f32[2,256,1024]{2,1,0:T(8,128)} %get-tuple-element.17) | copy-start | bytes 6291460
  171.7 4.0 %copy-start.1 = (bf16[2,256,1024]{2,1,0:T(8,128)(2,1)S(1)}, bf16[2,256,1024]{2,1,0:T(8,128)(2,1)}, u32[]{:S(2)}) copy-start(bf16[2,256,1024]{2,1,0:T(8,128)(2,1)} %get-tuple-element.18) | copy-start | bytes 3145732
  171.7 3.9 %copy-start.2 = (bf16[2,256,1024]{2,1,0:T(8,128)(2,1)S(1)}, bf16[2,256,1024]{2,1,0:T(8,128)(2,1)}, u32[]{:S(2)}) copy-start(bf16[2,256,1024]{2,1,0:T(8,128)(2,1)} %get-tuple-element.19) | copy-start | bytes 3145732
  175.7 1.8 %copy-start.3 = (bf16[128,1024]{1,0:T(8,128)(2,1)S(1)}, bf16[128,1024]{1,0:T(8,128)(2,1)}, u32[]{:S(2)}) copy-start(bf16[128,1024]{1,0:T(8,128)(2,1)} %get-tuple-element.24) | copy-start | bytes 786436
  175.7 2.5 %copy-start.4 = (f32[2,128]{1,0:T(2,128)S(1)}, f32[2,128]{1,0:T(2,128)}, u32[]{:S(2)}) copy-start(f32[2,128]{1,0:T(2,128)} %get-tuple-element.13) | copy-start | bytes 3076

commit v3 on v2

--- a/solution.py
+++ b/solution.py
@@ -456,33 +456,32 @@
     back_edge(0, ((1, 7), (2, 6)))
     last_passes(0, lambda: y_forward(1))
     weight_grads(0, 2)
+    weight_grads(0, 1)
+    weight_grads(0, 3)
     z_passes(1, (1, 7))
     gates_out(0)
     back_inner(0, inner_first)
-    weight_grads(0, 1)
-    weight_grads(0, 3)
     z_passes(1, (2, 6))
     weight_grads(0, 0)
+    y_relay(0)
     back_inner(0, inner_last)
     back_edge(0, edge_last)
     y_rest(1)
     compute(1, 0)
-    y_relay(0)
     compute(1, 1)
     back_edge(1, ((1, 7), (2, 6)))
-    last_passes(1, lambda: None)
+    last_passes(1, lambda: give_back(0))
     weight_grads(1, 2)
+    weight_grads(1, 1)
+    weight_grads(1, 3)
     back_inner(1, inner_first)
     gates_out(1)
-    give_back(0)
-    weight_grads(1, 1)
-    weight_grads(1, 3)
     back_inner(1, inner_last)
     back_edge(1, edge_last)
     weight_grads(1, 0)
+    y_relay(1)
+    give_back(1)
     y_final(0)
-    give_back(1)
-    y_relay(1)
     for e in range(2):
         for k, j in peers:
             ret_copy(e, k, j).wait_recv()

time: 181 us -> 174 us (0.961)
  Pallas kernels: 171 us -> 166 us
    pallas_call x1, Pallas kernels: 171 us -> 166 us  [per_device(): pl.pallas_call(kernel, out_shape=[jax.ShapeDtypeStruct(*of) for of in sha...]
where the time goes in v3:
time: 174 us; the launch traced here: 173 us
  Pallas kernels  166 us (95%)
  other arithmetic  5.74 us (3%)
    pallas_call x1, Pallas kernels, per_device(): pl.pallas_call(kernel, out_shape=[jax.ShapeDtypeStruct(*of) for of in sha...  166 us
    add x1, other arithmetic, per_device(): gwin = own_i + left_i.astype(F32) + right_i.astype(F32)  3.93 us

profile of v3, /device:TPU:1, one launch (start us, length us, event | category | flops | bytes accessed | tf_op | source)
XLA Modules:
  0.0 173.3 jit_solution(15027854822991568647)
XLA Ops:
  0.6 165.6 %moe_backward.1 = (bf16[128,1024]{1,0:T(8,128)(2,1)}, f32[2,128]{1,0:T(2,128)}, f32[2,1024,256]{2,1,0:T(8,128)}, f32[2,256,1024]{2,1,0:T(8,128)}, bf16[2,1024,25...) custom-call(bf16[128,1024]{1,0:T(8,128)(2,1)} %tok.1, ...), custom_call_target="tpu_custom_call" | custom-call | tf_op jit(solution)/shard_map/moe_backward/pallas_call | solution.py:529
  166.2 0.0 copy-start
  166.3 0.0 copy-start.1
  166.3 0.0 copy-start.2
  166.3 3.9 %convert_add_fusion.1 = f32[2,1024,256]{2,1,0:T(8,128)} fusion(bf16[2,1024,256]{2,1,0:T(8,128)(2,1)} %get-tuple-element.16, f32[2,1024,256]{2,1,0:T(8,128)} %get-tuple-element.14, bf16[2,1024,256]{2,1,0:T(8,128)(2,1)} %get-tuple-element.15), kind=kLoop, calls=%fused_computation.1 | loop fusion | flops 2097152 | bytes 6291456 | tf_op jit(solution)/shard_map/add | solution.py:540
  170.2 0.0 copy-done
  170.2 0.0 copy-done.1
  170.2 0.0 copy-done.2
  170.2 0.0 copy-start.3
  170.2 0.0 copy-start.4
  170.2 1.8 %convert_add_fusion = f32[2,256,1024]{2,1,0:T(8,128)} fusion(bf16[2,256,1024]{2,1,0:T(8,128)(2,1)S(1)} %copy-done.2, f32[2,256,1024]{2,1,0:T(8,128)S(1)} %copy-done, bf16[2,256,1024]{2,1,0:T(8,128)(2,1)S(1)} %copy-done.1), kind=kLoop, calls=%fused_computation | loop fusion | flops 2097152 | bytes 6291456 | tf_op jit(solution)/shard_map/add | solution.py:541
  172.1 0.0 copy-done.3
  172.1 0.7 copy.12
  172.8 0.0 copy-done.4
  172.8 0.6 copy.13
Async XLA Ops:
  166.2 4.0 %copy-start = (f32[2,256,1024]{2,1,0:T(8,128)S(1)}, f32[2,256,1024]{2,1,0:T(8,128)}, u32[]{:S(2)}) copy-start(f32[2,256,1024]{2,1,0:T(8,128)} %get-tuple-element.17) | copy-start | bytes 6291460
  166.3 4.0 %copy-start.1 = (bf16[2,256,1024]{2,1,0:T(8,128)(2,1)S(1)}, bf16[2,256,1024]{2,1,0:T(8,128)(2,1)}, u32[]{:S(2)}) copy-start(bf16[2,256,1024]{2,1,0:T(8,128)(2,1)} %get-tuple-element.18) | copy-start | bytes 3145732
  166.3 3.9 %copy-start.2 = (bf16[2,256,1024]{2,1,0:T(8,128)(2,1)S(1)}, bf16[2,256,1024]{2,1,0:T(8,128)(2,1)}, u32[]{:S(2)}) copy-start(bf16[2,256,1024]{2,1,0:T(8,128)(2,1)} %get-tuple-element.19) | copy-start | bytes 3145732
  170.2 1.8 %copy-start.3 = (bf16[128,1024]{1,0:T(8,128)(2,1)S(1)}, bf16[128,1024]{1,0:T(8,128)(2,1)}, u32[]{:S(2)}) copy-start(bf16[128,1024]{1,0:T(8,128)(2,1)} %get-tuple-element.24) | copy-start | bytes 786436
  170.2 2.5 %copy-start.4 = (f32[2,128]{1,0:T(2,128)S(1)}, f32[2,128]{1,0:T(2,128)}, u32[]{:S(2)}) copy-start(f32[2,128]{1,0:T(2,128)} %get-tuple-element.13) | copy-start | bytes 3076
